TPU v7x, 32 devices: a whole 2x2x4 slice. The times are simulated.
32 devices in a mesh: areal: 8 (over y, x, core), layer: 4 (over z).
Axes of the slice: x: 2, y: 2, z: 4, core: 2. Of those that a mesh axis runs over, the one named last changes fastest.
Arguments:
- pressure: float32 [8, 256, 1024], P(None, 'areal', 'layer'), may hold values from 0.7 to 1.4
- composition: float32 [9, 8, 256, 1024], P(None, None, 'areal', 'layer'), may hold values from 0.02 to 1
- mass_old: float32 [9, 8, 256, 1024], P(None, None, 'areal', 'layer'), may hold values from 0 to 0.3
- pore_volume: float32 [8, 256, 1024], P(None, 'areal', 'layer'), may hold values from 0.5 to 2
- trans_x: float32 [8, 256, 1024], P(None, 'areal', 'layer'), may hold values from 0.3 to 3
- trans_y: float32 [8, 256, 1024], P(None, 'areal', 'layer'), may hold values from 0.3 to 3
- trans_z: float32 [8, 256, 1024], P(None, 'areal', 'layer'), may hold values from 0.3 to 3
- volatility: float32 [9], replicated, may hold values from 1.5 to 3
- pressure_slope: float32 [9], replicated, may hold values from 0.2 to 1
- mixing: float32 [9, 9], replicated, may hold values from -3.5 to 3.5
- two_phase: int32 [4, 64], P(None, 'areal'), may hold values from 0 to 1, as said below
Outputs:
- residual: float32 [9, 8, 256, 1024], P(None, None, 'areal', 'layer')
- new_pressure: float32 [8, 256, 1024], P(None, 'areal', 'layer')
Inputs may be any that keep to these rules, and one draw needn't show every extreme that they name: `two_phase`: for each areal index, the 4 rows together flag exactly 16 of their bricks of that areal index, and one of the rows flags all of its 8 bricks of that areal index.
All inputs are finite; a program needn't handle non-finite values.
Results may differ from a plain program's by a relative error of at most 0.0003.
Values sent between devices are 32-bit elements; how exact they have to be, the bound alone decides.
No kernel may reach another device: no remote copies, remote signals or barrier semaphores. Data moves between devices by JAX's collectives and lax.ppermute only.
A program may use at most 128 MiB of HBM per device.

v0:
```python
import jax
import jax.numpy as jnp
from jax import lax
from jax.experimental import pallas as pl
from jax.experimental.pallas import tpu as pltpu
from jax.sharding import PartitionSpec as P

SS_ITERS = 3
RR_ITERS = 3
LIGHT = 4
COMPS = 9
FIELDS = 16
MOB, PRESS, TX, TY, TZ, PORE, ACC = range(COMPS, FIELDS)
UNITS = (MOB, PRESS, TX, (0, 1), (2, 3), (4, 5), (6, 7), (8, TY), (TZ, PORE), (ACC, ACC))
DEPTH_SLOTS = 4
TIME_STEP = 4.0
COMPRESS = 0.2
VAPOUR_WEIGHT = 1.0 / 0.25
LANES = 128
ROWS = 8
MIB = 1024 * 1024
PART = (COMPS + 1) * ROWS
DEEP = 256


def rcp(x):
    return pltpu.reciprocal(x, approx=True)


def total_of(terms):
    terms = list(terms)
    while len(terms) > 1:
        terms = [a + b for a, b in zip(terms[::2], terms[1::2])] + (
            [terms[-1]] if len(terms) % 2 else []
        )
    return terms[0]


def split(x):
    high = x.astype(jnp.bfloat16)
    return high, (x - high.astype(jnp.float32)).astype(jnp.bfloat16)


def mixing_operand(mix_ref):
    shape = (ROWS, DEEP)
    lane, row = lane_of(shape), row_of(shape)
    part = lax.div(lane, PART)
    within = lane - PART * part
    column = lax.div(within, ROWS)
    on = (within - ROWS * column == row) & (part < 3)
    blocks = []
    for i in range(COMPS):
        value = jnp.zeros(shape, jnp.float32)
        for j in range(COMPS):
            value = jnp.where(column == j, 2.0 * mix_ref[i, j], value)
        high, low = split(value)
        value = jnp.where(part == 2, low.astype(jnp.float32), high.astype(jnp.float32))
        blocks.append(jnp.where(on, value, 0.0))
    blocks.append(jnp.zeros(shape, jnp.float32))
    return jnp.concatenate(blocks, axis=0).astype(jnp.bfloat16)


def mixed(operand, spread):
    shape = spread[0].shape
    high, low = split(jnp.concatenate(spread + [jnp.zeros(shape, jnp.float32)], axis=0))
    tail = jnp.zeros((DEEP - 3 * PART, shape[1]), jnp.bfloat16)
    out = jnp.dot(
        operand,
        jnp.concatenate([high, low, high, tail], axis=0),
        preferred_element_type=jnp.float32,
    )
    return [out[ROWS * i : ROWS * (i + 1)] for i in range(COMPS)]


def flash(feed, pressure, signed, slope, operand):
    log_press = jnp.log(pressure)
    half_base = [0.5 * signed[i] - (0.5 * slope[i]) * log_press for i in range(COMPS)]
    spread = None
    for outer in range(SS_ITERS):
        if outer == 0:
            half_log = half_base
        else:
            mix = mixed(operand, spread)
            half_log = [half_base[i] - 0.5 * jnp.tanh(mix[i]) for i in range(COMPS)]
        t = [jnp.tanh(half_log[i]) for i in range(COMPS)]
        u = [rcp(t[i]) for i in range(COMPS)]
        psi = None
        for inner in range(RR_ITERS):
            q = t if inner == 0 else [rcp(u[i] + psi) for i in range(COMPS)]
            part = [feed[i] * q[i] for i in range(COMPS)]
            step = total_of(part) * rcp(total_of(part[i] * q[i] for i in range(COMPS)))
            psi = jnp.clip(step if inner == 0 else psi + step, -1.0, 1.0)
        spread = [feed[i] * rcp(u[i] + psi) for i in range(COMPS)]
    liquid_part = (0.25 * (1.0 - psi)) * (1.0 - psi)
    vapour_part = (0.25 * VAPOUR_WEIGHT * (1.0 + psi)) * (1.0 + psi)
    both, apart = vapour_part + liquid_part, vapour_part - liquid_part
    return [spread[i] * (both * u[i] + apart) for i in range(COMPS)]


def parameters(vol_ref, slope_ref):
    signed = [vol_ref[i] if i < LIGHT else -vol_ref[i] for i in range(COMPS)]
    return signed, [slope_ref[i] for i in range(COMPS)]


def lane_of(shape):
    return lax.broadcasted_iota(jnp.int32, shape, len(shape) - 1)


def row_of(shape):
    return lax.broadcasted_iota(jnp.int32, shape, len(shape) - 2)


class Rows:
    def __init__(self, edge, inner):
        self.edge, self.inner = edge, inner

    def __getitem__(self, at):
        at = at if isinstance(at, tuple) else (at,)
        edge = self.edge[at]
        return jnp.concatenate([edge[:ROWS], self.inner[at], edge[ROWS:]], axis=0)


def pack_rows(field, low, out_ref, depth):
    row = None
    for n in range(0, len(UNITS), 2):
        for pair in range(depth // 2):
            tile = None
            for z in (2 * pair, 2 * pair + 1):
                order = (1, 0) if low else (0, 1)
                for which in order:
                    unit = UNITS[n + which]
                    at = 4 * (z % 2) + (2 if low == (which == 0) else 0)
                    first = 0 if low else ROWS - 1
                    if isinstance(unit, tuple):
                        a, b = unit
                        pieces = [(at, a, at - first), (at + 1, b, at + 1 - first)]
                        if not low:
                            pieces = [(at, b, at - first), (at + 1, a, at + 1 - first)]
                    else:
                        pieces = [(at, unit, at if low else at + 2)]
                    for start, k, turn in pieces:
                        here = field(k, z)
                        if row is None:
                            row = row_of(here.shape)
                        if turn % ROWS:
                            here = pltpu.roll(here, turn % ROWS, 0)
                        tile = here if tile is None else jnp.where(row < start, tile, here)
            out_ref[n // 2, pl.ds(pair * ROWS, ROWS), :] = tile


def row_tiles(one, two, wanted, start=0, stop=None):
    shape = one.shape[1:]
    upper = row_of(shape) % DEPTH_SLOTS < 2
    tile_row = row_of((ROWS, shape[1]))
    stop = stop or shape[0] // DEPTH_SLOTS
    tiles = {}
    for n, unit in enumerate(UNITS):
        fields = unit if isinstance(unit, tuple) else (unit,)
        if not any(k in wanted for k in fields):
            continue
        up, down = by_side("areal", one[n // 2], two[n // 2])
        if n % 2:
            up, down = pltpu.roll(up, shape[0] - 2, 0), pltpu.roll(down, 2, 0)
        both = jnp.where(upper, up, down)
        for z in range(start, stop):
            at = (z // 2) * ROWS
            tile = pltpu.roll(both[at : at + ROWS], 6 - 4 * (z % 2), 0)
            if fields[0] in wanted:
                tiles.setdefault(fields[0], []).append(tile)
            if fields[-1] in wanted and fields[-1] != fields[0]:
                other = jnp.where(tile_row < 4, pltpu.roll(tile, ROWS - 1, 0), pltpu.roll(tile, 1, 0))
                tiles.setdefault(fields[-1], []).append(other)
    return tiles


def pack_columns(rows_one, rows_two, *refs):
    (
        press, tx, ty, tz, pore, edge_mob, _, edge_mob_sum, edge_acc_sum, mob, _, mob_sum, acc_sum,
        one_ref, two_ref, own_ref,
    ) = refs
    depth, rows, width = press.shape
    shape = (rows + ROWS, LANES)
    lane = lane_of(shape)
    mob, mob_sum, acc_sum = (
        Rows(*both) for both in ((edge_mob, mob), (edge_mob_sum, mob_sum), (edge_acc_sum, acc_sum))
    )
    corner_fields = {MOB: mob_sum, PRESS: press, TX: tx, TY: ty}
    others = {TZ: tz, PORE: pore, ACC: acc_sum, **corner_fields}
    corners = row_tiles(rows_one, rows_two, corner_fields)
    nothing = jnp.zeros((ROWS, LANES), jnp.float32)
    for tile in range(FIELDS // 4):
        packed = jnp.zeros(shape, jnp.float32)
        for quarter in range(4):
            k = 4 * tile + quarter
            for z in range(depth):
                plane = mob[k, z] if k < COMPS else others[k][z]
                first, last = plane[:, :LANES], plane[:, -LANES:]
                at = 32 * quarter + 4 * z
                both = jnp.where(lane_of(first.shape) < LANES // 2, first, last)
                if k < COMPS:
                    both = pltpu.roll(both, at + 2, 1)
                    on = (lane_of(first.shape) >= at + 1) & (lane_of(first.shape) < at + 3)
                    packed = jnp.concatenate([jnp.where(on, both, packed[:rows]), nothing], axis=0)
                    continue
                end = nothing
                if k in corner_fields:
                    end = corners[k][z]
                    end = jnp.where(lane_of(end[:, :LANES].shape) < LANES // 2, end[:, :LANES], end[:, -LANES:])
                both = pltpu.roll(jnp.concatenate([both, end], axis=0), (at + 2) % LANES, 1)
                packed = jnp.where((lane >= at) & (lane < at + 4), both, packed)
        own_ref[:, tile * LANES : (tile + 1) * LANES] = packed
    odd = lax.axis_index("layer") % 2 == 1
    half = FIELDS // 8
    for n in range(half):
        near, far = (own_ref[:, t * LANES : (t + 1) * LANES] for t in (n, n + half))
        upward = jnp.where(lane % 4 < 2, near, pltpu.roll(far, 2, 1))
        downward = jnp.where(lane % 4 < 2, pltpu.roll(near, LANES - 2, 1), far)
        one_ref[:, n * LANES : (n + 1) * LANES] = jnp.where(odd, downward, upward)
        two_ref[:, n * LANES : (n + 1) * LANES] = jnp.where(odd, upward, downward)


def spread_fields(tiles):
    fields = []
    for tile in tiles:
        for quarter in range(4):
            turn = (LANES - 32 * quarter) % LANES
            fields.append(pltpu.roll(tile, turn, 1) if turn else tile)
    return fields


def side_fields(one, two):
    lane = lane_of((one.shape[0], LANES))
    near, far = [], []
    for n in range(FIELDS // 8):
        span = slice(n * LANES, (n + 1) * LANES)
        left, right = by_side("layer", one[:, span], two[:, span])
        near.append(jnp.where(lane % 4 < 2, left, pltpu.roll(right, 2, 1)))
        far.append(jnp.where(lane % 4 < 2, pltpu.roll(left, LANES - 2, 1), right))
    return spread_fields(near + far)


def flash_rows(source, target, tile_row, flags, vol, slope, operand, comp, press, pore, mass, outs, ready=None):
    mob_ref, acc_ref, mob_sum, acc_sum = outs
    layer = lax.axis_index("layer")
    depth, _, width = press.shape

    def beside(ref, *lead):
        return jnp.concatenate([ref[(*lead, z, source)] for z in range(depth)], axis=1)

    def store(ref, value, *lead):
        for z in range(depth):
            ref[(*lead, z, target)] = value[:, z * width : (z + 1) * width]

    raw = [beside(comp, i) for i in range(COMPS)]
    inverse = rcp(total_of(raw))
    feed = [raw[i] * inverse for i in range(COMPS)]
    first, last = flags[layer, 2 * tile_row], flags[layer, 2 * tile_row + 1]

    @pl.when(first + last > 0)
    def _():
        signed, slopes = parameters(vol, slope)
        two = flash(feed, beside(press), signed, slopes, operand[...])
        marked = jnp.where(row_of(feed[0].shape) < ROWS // 2, first, last) > 0
        mobility = [jnp.where(marked, two[i], feed[i]) for i in range(COMPS)]
        for i in range(COMPS):
            store(mob_ref, mobility[i], i)
        store(mob_sum, total_of(mobility))

    @pl.when(first + last == 0)
    def _():
        for i in range(COMPS):
            store(mob_ref, feed[i], i)
        store(mob_sum, total_of(feed))

    if ready:
        ready()
    volume = beside(pore)
    acc = [volume * feed[i] - beside(mass, i) for i in range(COMPS)]
    for i in range(COMPS):
        store(acc_ref, acc[i], i)
    store(acc_sum, total_of(acc))


def edge_cells(
    flags_in, vol_in, slope_in, mix_in, comp, press, pore, mass, tx, ty, tz,
    mob_ref, acc_ref, mob_sum, acc_sum, one_ref, two_ref, operand, comp_i, press_i, pore_i, mass_i,
    flags, vol, slope, mix, comp_s, press_s, pore_s, mass_s, tx_s, ty_s, tz_s, sems, scalar_sems,
):
    depth, rows, _ = press.shape
    fetched = (
        (comp, comp_s), (press, press_s), (pore, pore_s), (mass, mass_s), (tx, tx_s), (ty, ty_s), (tz, tz_s)
    )

    ahead = (comp_i, press_i, pore_i, mass_i)

    def fetch(end, n):
        source, slot = fetched[n]
        at = pl.ds(end * (rows - ROWS), ROWS) if end < 2 else pl.ds(ROWS, rows - 2 * ROWS)
        return pltpu.make_async_copy(
            source.at[:, :, at, :] if len(source.shape) == 4 else source.at[:, at, :],
            slot.at[end] if end < 2 else ahead[n],
            sems.at[end, n],
        )

    scalars = [
        pltpu.make_async_copy(source, slot, scalar_sems.at[n])
        for n, (source, slot) in enumerate(
            ((flags_in, flags), (vol_in, vol), (slope_in, slope), (mix_in, mix))
        )
    ]
    early, late = (0, 1), range(2, len(fetched))
    for copy in scalars:
        copy.start()
    for n in early:
        fetch(0, n).start()
    for copy in scalars:
        copy.wait()
    operand[...] = mixing_operand(mix)
    odd = lax.axis_index("areal") % 2 == 1
    for end in range(2):
        for n in early:
            fetch(end, n).wait()
        if end == 0:
            for n in late:
                fetch(0, n).start()
            for n in range(len(fetched)):
                fetch(1, n).start()
        else:
            for n in range(len(ahead)):
                fetch(2, n).start()

        def ready():
            for n in late:
                fetch(end, n).wait()

        target = slice(end * ROWS, (end + 1) * ROWS)
        flash_rows(
            slice(None), target, end * (rows // ROWS - 1), flags, vol, slope, operand,
            *(slot.at[end] for _, slot in fetched[:4]), (mob_ref, acc_ref, mob_sum, acc_sum), ready,
        )

        def field(k, z):
            if k < COMPS:
                here = mob_ref[k, z, target]
            elif k in (MOB, ACC):
                here = (mob_sum if k == MOB else acc_sum)[z, target]
            else:
                here = {PRESS: press_s, TX: tx_s, TY: ty_s, TZ: tz_s, PORE: pore_s}[k][end, z]
            return here

        for turn, ref in enumerate((one_ref, two_ref)):
            @pl.when(odd == (end == turn))
            def _():
                pack_rows(field, end == 0, ref, depth)

    for n in range(len(ahead)):
        fetch(2, n).wait()


def inner_cells(flags, vol, slope, operand, comp, press, pore, mass, *outs):
    def tile(t, carry):
        at = pl.ds(pl.multiple_of(t * ROWS, ROWS), ROWS)
        flash_rows(at, at, t + 1, flags, vol, slope, operand, comp, press, pore, mass, outs)
        return carry

    lax.fori_loop(0, press.shape[1] // ROWS, tile, 0)


def by_side(axis, one, two):
    odd = lax.axis_index(axis) % 2 == 1
    return jnp.where(odd, one, two), jnp.where(odd, two, one)


def by_pairs(count, body):
    def pair(t, carry):
        body(2 * t)
        body(2 * t + 1)
        return carry

    lax.fori_loop(0, count // 2, pair, 0)


def near_residual(
    rows_one, rows_two, press, tx, ty, tz, pore,
    edge_mob, edge_acc, edge_mob_sum, edge_acc_sum, mob, acc, mob_sum, acc_sum,
    out_ref, total_ref, diagonal_ref, c_x, c_y, c_z,
    rows_h, fields_h, g_x, g_y, g_z,
):
    depth, rows, width = press.shape
    areal, areals = lax.axis_index("areal"), lax.axis_size("areal")
    tall = rows + ROWS
    full = (tall, width)
    own = slice(0, rows)
    mob, acc, mob_sum, acc_sum = (
        Rows(*both)
        for both in ((edge_mob, mob), (edge_acc, acc), (edge_mob_sum, mob_sum), (edge_acc_sum, acc_sum))
    )
    fields = {MOB: mob_sum, PRESS: press, TX: tx, TY: ty, TZ: tz, PORE: pore, ACC: acc_sum}
    tiles = row_tiles(rows_one, rows_two, range(FIELDS))
    for z in range(depth):
        for i in range(COMPS):
            rows_h[i, z] = tiles[i][z]
        for n, k in enumerate(fields):
            fields_h[n, z] = tiles[k][z]

    end_x = (row_of(full) == rows - 1) & (areal == areals - 1)
    end_y = lane_of(full) == width - 1
    scale = 0.5 * TIME_STEP
    c_z[0] = jnp.zeros(full, jnp.float32)
    g_z[0] = jnp.zeros((rows, width), jnp.float32)

    def update(z):
        m, p, x, y, zz, volume, total = (
            jnp.concatenate([ref[z], fields_h[n, z]], axis=0) for n, ref in enumerate(fields.values())
        )
        up, down = jnp.minimum(z + 1, depth - 1), jnp.maximum(z - 1, 0)
        p_up = jnp.concatenate([press[up], fields_h[1, up]], axis=0)
        p_down = jnp.concatenate([press[down], fields_h[1, down]], axis=0)
        m_up = jnp.concatenate([mob_sum[up], fields_h[0, up]], axis=0)
        strength_x = jnp.where(end_x, 0.0, scale * x)
        strength_y = jnp.where(end_y, 0.0, scale * y)
        strength_z = jnp.where(z < depth - 1, scale, 0.0) * zz
        dx = p - pltpu.roll(p, tall - 1, 0)
        dy = p - pltpu.roll(p, width - 1, 1)
        dz = p - p_up
        cx = strength_x * (m + pltpu.roll(m, tall - 1, 0))
        cy = strength_y * (m + pltpu.roll(m, width - 1, 1))
        cz = strength_z * (m + m_up)
        cz_low = c_z[z]
        gx = strength_x * dx
        g_x[0, z], g_x[1, z] = gx[own], -pltpu.roll(gx, 1, 0)[own]
        g_y[z], g_z[z + 1] = (strength_y * dy)[own], (strength_z * dz)[own]
        c_x[z], c_y[z], c_z[z + 1] = cx, cy, cz
        fx, fy = cx * dx, cy * dy
        total_ref[z] = (
            total
            + (fx - pltpu.roll(fx, 1, 0))
            + (fy - pltpu.roll(fy, 1, 1))
            + (cz * dz + cz_low * (p - p_down))
        )
        diagonal_ref[z] = (
            COMPRESS * volume
            + (cx + pltpu.roll(cx, 1, 0))
            + (cy + pltpu.roll(cy, 1, 1))
            + (cz + cz_low)
        )

    by_pairs(depth, update)

    def residual(z):
        down, up = jnp.maximum(z - 1, 0), jnp.minimum(z + 1, depth - 1)
        gx, gx_low, gy, gz, gz_low = g_x[0, z], g_x[1, z], g_y[z], g_z[z + 1], -g_z[z]
        gy_low = -pltpu.roll(gy, 1, 1)
        middle = (gx + gx_low) + (gy + gy_low) + (gz + gz_low)
        for i in range(COMPS):
            here = mob[i, z]
            tall_here = jnp.concatenate([here, rows_h[i, z]], axis=0)
            out_ref[i, z] = (
                acc[i, z]
                + middle * here
                + gx * pltpu.roll(tall_here, tall - 1, 0)[own]
                + gx_low * pltpu.roll(tall_here, 1, 0)[own]
                + gy * pltpu.roll(here, width - 1, 1)
                + gy_low * pltpu.roll(here, 1, 1)
                + gz * mob[i, up]
                + gz_low * mob[i, down]
            )

    by_pairs(depth, residual)


def finish(
    columns_one, columns_two, packet, press, total_in, diagonal_in, c_x, c_y, c_z, edge_mob, mob, near,
    res_ref, new_ref,
    side_h, edge_h, first, total_ref, inverse_ref, res_s, sems,
):
    depth, rows, width = press.shape
    layer, layers = lax.axis_index("layer"), lax.axis_size("layer")
    areal, areals = lax.axis_index("areal"), lax.axis_size("areal")
    tall = rows + ROWS
    lane = lane_of((tall, LANES))
    at_first, at_last = lane == 0, lane == LANES - 1
    low, high = slice(0, LANES), slice(width - LANES, width)
    FLUX, COUPLE, FACE, NEXT = range(4)
    mob = Rows(edge_mob, mob)

    def edges(which, z):
        both = pltpu.roll(edge_h[which], LANES - 1 - 4 * z, 1)
        return jnp.where(at_first, both, 0.0), jnp.where(at_last, both, 0.0)

    halo = side_fields(columns_one, columns_two)
    here = spread_fields([packet[:, t : t + LANES] for t in range(0, FIELDS * 32, LANES)])
    is_left = lane % 4 == 1
    for i in range(COMPS):
        cells = halo[i][:rows]
        side_h[i] = jnp.where(is_left[:rows], pltpu.roll(cells, LANES - 1, 1), pltpu.roll(cells, 1, 1))
    scale = 0.5 * TIME_STEP

    def turned(x, by):
        return pltpu.roll(x, by % LANES, 1)

    def outer(x):
        return jnp.where(is_left, turned(x, 1), turned(x, -1))

    def inner(x):
        return jnp.where(is_left, turned(x, -1), turned(x, 1))

    m, p = halo[MOB], halo[PRESS]
    strength = scale * halo[TY]
    own_strength = jnp.where(layer < layers - 1, scale, 0.0) * here[TY]
    c_out = jnp.where(is_left, turned(strength, 1), strength) * (m + outer(m))
    s_in = jnp.where(is_left, strength, turned(own_strength, 1))
    c_in = s_in * (m + inner(here[MOB]))
    d_in = p - inner(here[PRESS])
    end_x = (row_of(lane.shape) == rows - 1) & (areal == areals - 1)
    cx = jnp.where(end_x, 0.0, scale * halo[TX]) * (m + pltpu.roll(m, tall - 1, 0))
    cz = jnp.where(lane < 4 * (depth - 1), scale * halo[TZ], 0.0) * (m + turned(m, -4))
    fx = cx * (p - pltpu.roll(p, tall - 1, 0))
    fz = cz * (p - turned(p, -4))
    total = (
        halo[ACC]
        + (c_out * (p - outer(p)) + c_in * d_in)
        + (fx - pltpu.roll(fx, 1, 0))
        + (fz - turned(fz, 4))
    )
    diagonal = (
        COMPRESS * halo[PORE] + (c_out + c_in) + (cx + pltpu.roll(cx, 1, 0)) + (cz + turned(cz, 4))
    )
    usable = diagonal > 0.0
    beside = jnp.where(usable, -total * rcp(jnp.where(usable, diagonal, 1.0)), 0.0)
    for which, value in (
        (FLUX, -c_in * d_in), (COUPLE, c_in), (FACE, -s_in * d_in), (NEXT, c_in * beside)
    ):
        edge_h[which] = jnp.where(is_left, value, turned(value, -2))

    def leave(z):
        return pltpu.make_async_copy(res_s.at[:, z], res_ref.at[:, z], sems.at[z])

    def update(z):
        faces = [face[:rows] for face in edges(FACE, z)]
        for i in range(COMPS):
            side = pltpu.roll(side_h[i], LANES - 2 - 4 * z, 1)
            cells = mob[i, z]
            for span, face in zip((low, high), faces):
                res_s[i, z, :, span] = near[i, z, :, span] + face * (cells[:, span] + side)
        leave(z).start()
        flux, couple = edges(FLUX, z), edges(COUPLE, z)
        for n, span in enumerate((low, high)):
            total = total_in[z, :, span] + flux[n]
            diagonal = diagonal_in[z, :, span] + couple[n]
            usable = diagonal > 0.0
            inverse = rcp(jnp.where(usable, diagonal, 1.0))
            first[z, :, span] = jnp.where(usable, -total * inverse, 0.0)
            total_ref[z, :, span] = total[:rows]
            inverse_ref[z, :, span] = inverse[:rows]

    by_pairs(depth, update)

    def second(z):
        here = first[z]
        up, down = jnp.minimum(z + 1, depth - 1), jnp.maximum(z - 1, 0)
        cx, cy = c_x[z], c_y[z, :rows]
        own = here[:rows]
        gathered = (
            (cx * pltpu.roll(here, tall - 1, 0))[:rows]
            + pltpu.roll(cx * here, 1, 0)[:rows]
            + cy * pltpu.roll(own, width - 1, 1)
            + pltpu.roll(cy * own, 1, 1)
            + (c_z[z + 1, :rows] * first[up, :rows] + c_z[z, :rows] * first[down, :rows])
            - total_ref[z]
        )
        beyond = edges(NEXT, z)
        for n, span in enumerate((low, high)):
            new_ref[z, :, span] = press[z, :, span] + inverse_ref[z, :, span] * (
                gathered[:, span] + beyond[n][:rows]
            )

    by_pairs(depth, second)

    def left(z):
        leave(z).wait()

    by_pairs(depth, left)


def on_device(
    pressure, composition, mass_old, pore_volume, trans_x, trans_y, trans_z,
    volatility, pressure_slope, mixing, two_phase,
):
    depth, rows, width = pressure.shape
    f32 = jnp.float32
    smem = pl.BlockSpec(memory_space=pltpu.SMEM)
    vmem = pl.BlockSpec(memory_space=pltpu.VMEM)
    def params(mib):
        return pltpu.CompilerParams(vmem_limit_bytes=mib * MIB)

    scalars = (two_phase, volatility, pressure_slope, mixing)

    def swapped(block, axis, first):
        count = lax.axis_size(axis)
        pairs = [(i, i + 1) for i in range(first, count - 1, 2)]
        return lax.ppermute(block, axis, pairs + [(j, i) for i, j in pairs])

    whole = jax.ShapeDtypeStruct((COMPS, depth, rows, width), f32)
    sums = jax.ShapeDtypeStruct((depth, rows, width), f32)
    packed = jax.ShapeDtypeStruct((len(UNITS) // 2, DEPTH_SLOTS * depth, width), f32)
    fields = (composition, pressure, pore_volume, mass_old, trans_x, trans_y, trans_z)

    def parts(count):
        planes = jax.ShapeDtypeStruct((COMPS, depth, count, width), f32)
        plane = jax.ShapeDtypeStruct((depth, count, width), f32)
        return [planes, planes, plane, plane]

    between = [jax.ShapeDtypeStruct((*x.shape[:-2], rows - 2 * ROWS, width), f32) for x in fields[:4]]
    *results, operand, comp, press, pore, mass = pl.pallas_call(
        edge_cells,
        in_specs=[pl.BlockSpec(memory_space=pl.ANY)] * (4 + len(fields)),
        out_specs=[vmem] * 11,
        out_shape=parts(2 * ROWS)
        + [packed, packed, jax.ShapeDtypeStruct((PART, DEEP), jnp.bfloat16), *between],
        scratch_shapes=[pltpu.SMEM(x.shape, x.dtype) for x in scalars]
        + [pltpu.VMEM((2, *x.shape[:-2], ROWS, width), f32) for x in fields]
        + [pltpu.SemaphoreType.DMA((3, len(fields))), pltpu.SemaphoreType.DMA((4,))],
        compiler_params=params(24),
        name="edge_cells",
    )(*(pltpu.with_memory_space_constraint(x, pltpu.HBM) for x in (*scalars, *fields)))
    *edge, one, two = results
    rows_two = swapped(two, "areal", 1)
    rows_one = swapped(one, "areal", 0)
    cells = rows * depth * width
    inner = pl.pallas_call(
        inner_cells,
        in_specs=[smem] * 3 + [vmem] * 5,
        out_specs=[vmem] * 4,
        out_shape=parts(rows - 2 * ROWS),
        compiler_params=params(24),
        cost_estimate=pl.CostEstimate(
            flops=450 * cells, transcendentals=95 * cells, bytes_accessed=2 * 39 * cells
        ),
        name="inner_cells",
    )(*scalars[:3], operand, comp, press, pore, mass)
    planes_of = (pressure, trans_x, trans_y, trans_z, pore_volume)

    narrow = jax.ShapeDtypeStruct((rows + ROWS, FIELDS * 16), f32)
    one, two, packet = pl.pallas_call(
        pack_columns,
        in_specs=[vmem] * 15,
        out_specs=[vmem] * 3,
        out_shape=[narrow, narrow, jax.ShapeDtypeStruct((rows + ROWS, FIELDS * 32), f32)],
        compiler_params=params(24),
        name="pack_columns",
    )(rows_one, rows_two, *planes_of, *edge, *inner)
    columns_one = swapped(one, "layer", 0)
    columns_two = swapped(two, "layer", 1)

    tall = jax.ShapeDtypeStruct((depth, rows + ROWS, width), f32)
    above_faces = jax.ShapeDtypeStruct((depth + 1, rows + ROWS, width), f32)
    near, *sweep = pl.pallas_call(
        near_residual,
        in_specs=[vmem] * 15,
        out_specs=[vmem] * 6,
        out_shape=[whole, tall, tall, tall, tall, above_faces],
        scratch_shapes=[
            pltpu.VMEM((COMPS, depth, ROWS, width), f32),
            pltpu.VMEM((FIELDS - COMPS, depth, ROWS, width), f32),
            pltpu.VMEM((2, depth, rows, width), f32),
            pltpu.VMEM((depth, rows, width), f32),
            pltpu.VMEM((depth + 1, rows, width), f32),
        ],
        compiler_params=params(24),
        cost_estimate=pl.CostEstimate(flops=150 * cells, transcendentals=0, bytes_accessed=4 * 31 * cells),
        name="near_residual",
    )(rows_one, rows_two, *planes_of, *edge, *inner)

    return pl.pallas_call(
        finish,
        in_specs=[vmem] * 12,
        out_specs=[pl.BlockSpec(memory_space=pl.ANY), vmem],
        out_shape=[whole, sums],
        scratch_shapes=[
            pltpu.VMEM((COMPS, rows, LANES), f32),
            pltpu.VMEM((4, rows + ROWS, LANES), f32),
            pltpu.VMEM((depth, rows + ROWS, width), f32),
            pltpu.VMEM((depth, rows, width), f32),
            pltpu.VMEM((depth, rows, width), f32),
            pltpu.VMEM((COMPS, depth, rows, width), f32),
            pltpu.SemaphoreType.DMA((depth,)),
        ],
        compiler_params=params(24),
        name="finish",
    )(columns_one, columns_two, packet, pressure, *sweep, edge[0], inner[0], near)


def solution(mesh):
    placed = (
        P(None, "areal", "layer"),
        P(None, None, "areal", "layer"),
        P(None, None, "areal", "layer"),
        P(None, "areal", "layer"),
        P(None, "areal", "layer"),
        P(None, "areal", "layer"),
        P(None, "areal", "layer"),
        P(),
        P(),
        P(),
        P(None, "areal"),
    )
    return jax.shard_map(
        on_device,
        mesh=mesh,
        in_specs=placed,
        out_specs=(P(None, None, "areal", "layer"), P(None, "areal", "layer")),
        check_vma=False,
    )
```

profile of v0, /device:TPU:12, one launch (start us, length us, event | category | flops | bytes accessed | tf_op | source)
XLA Modules:
  0.0 27.7 jit_solution(8172830295124657526)
XLA Ops:
  0.6 0.0 copy-start.5
  0.6 0.0 copy-start.7
  0.7 0.0 copy-start.6
  0.7 5.7 %edge_cells.1 = (f32[9,8,16,256]{3,2,1,0:T(8,128)S(1)}, f32[9,8,16,256]{3,2,1,0:T(8,128)S(1)}, f32[8,16,256]{2,1,0:T(8,128)S(1)}, f32[8,16,256]{2,1,0:T(8,128)S(...) custom-call(s32[4,8]{1,0:T(4,128)} %flags.1, ...), custom_call_target="tpu_custom_call" | custom-call | tf_op jit(solution)/shard_map/edge_cells/pallas_call | solution.py:615
  6.4 0.1 collective-permute-start
  6.5 3.4 %collective-permute-start.1 = (f32[5,32,256]{2,1,0:T(8,128)S(1)}, f32[5,32,256]{2,1,0:T(8,128)S(1)}, u32[]{:S(2)}, u32[]{:S(2)}) collective-permute-start(f32[5,32,256]{2,1,0:T(8,128)S(1)} %get-tuple-element.27), channel_id=1, source_target_pairs={{4,8},{12,16},{20,24},{8,4},{16,12},{24,20},{5,9},{13,17},{21,25},... | collective-permute-start | bytes 491528 | tf_op jit(solution)/shard_map/ppermute | solution.py:602
  9.9 0.0 copy-done.5
  9.9 0.0 copy-done.7
  10.0 0.0 copy-done.6
  10.0 0.0 copy-start
  10.0 0.0 copy-start.1
  10.0 0.0 copy-start.2
  10.0 0.0 copy-start.3
  10.0 0.0 copy-start.4
  10.0 1.1 %inner_cells.1 = (f32[9,8,16,256]{3,2,1,0:T(8,128)S(1)}, f32[9,8,16,256]{3,2,1,0:T(8,128)S(1)}, f32[8,16,256]{2,1,0:T(8,128)S(1)}, f32[8,16,256]{2,1,0:T(8,128)S(1)}) custom-call(s32[4,8]{1,0:T(4,128)S(1)} %copy-done.5, f32[9]{0:T(128)S(1)} %copy-done.6, f32[9]{0:T(128)S(1)} %copy-done.7, bf16[80,256]{1,0:T(8,128)(2,1)S(1)} %get-tuple-element.32.operand, ...), custom_call_target="tpu_custom_call" | custom-call | flops 29491200 | bytes 5111808 | tf_op jit(solution)/shard_map/inner_cells/pallas_call | solution.py:631
  11.1 0.0 collective-permute-done.rows_one
  11.1 3.9 %collective-permute-done.1.rows_two = f32[5,32,256]{2,1,0:T(8,128)S(1)} collective-permute-done((f32[5,32,256]{2,1,0:T(8,128)S(1)}, f32[5,32,256]{2,1,0:T(8,128)S(1)}, u32[]{:S(2)}, u32[]{:S(2)}) %collective-permute-start.1) | collective-permute-done | bytes 163872 | tf_op jit(solution)/shard_map/ppermute | solution.py:602
  15.0 0.0 copy-done
  15.0 0.0 copy-done.1
  15.0 0.0 copy-done.2
  15.0 0.0 copy-done.3
  15.0 0.0 copy-done.4
  15.0 0.8 %pack_columns.1 = (f32[40,256]{1,0:T(8,128)S(1)}, f32[40,256]{1,0:T(8,128)S(1)}, f32[40,512]{1,0:T(8,128)S(1)}) custom-call(f32[5,32,256]{2,1,0:T(8,128)S(1)} %collective-permute-done.rows_one, f32[5,32,256]{2,1,0:T(8,128)S(1)} %collective-permute-done.1.rows_two, f32[8,32,256]{2,1,0:T(8,128)S(1)} %copy-done, f32[8,32,256]{2,1,0:T(8,128)S(1)} %copy-done.2, ...), custom_call_target="tpu_custom_call" | custom-call | tf_op jit(solution)/shard_map/pack_columns/pallas_call | solution.py:645
  15.8 0.4 %collective-permute-start.2 = (f32[40,256]{1,0:T(8,128)S(1)}, f32[40,256]{1,0:T(8,128)S(1)}, u32[]{:S(2)}, u32[]{:S(2)}) collective-permute-start(f32[40,256]{1,0:T(8,128)S(1)} %get-tuple-element.41), channel_id=1, source_target_pairs={{0,1},{2,3},{1,0},{3,2},{4,5},{6,7},{5,4},{7,6},{8,9},{10,11},{9,8... | collective-permute-start | bytes 122888 | tf_op jit(solution)/shard_map/ppermute | solution.py:602
  16.2 5.2 %collective-permute-start.3 = (f32[40,256]{1,0:T(8,128)S(1)}, f32[40,256]{1,0:T(8,128)S(1)}, u32[]{:S(2)}, u32[]{:S(2)}) collective-permute-start(f32[40,256]{1,0:T(8,128)S(1)} %get-tuple-element.42), channel_id=1, source_target_pairs={{1,2},{2,1},{5,6},{6,5},{9,10},{10,9},{13,14},{14,13},{17,18},{18,... | collective-permute-start | bytes 122888 | tf_op jit(solution)/shard_map/ppermute | solution.py:602
  21.4 3.5 %near_residual.1 = (f32[9,8,32,256]{3,2,1,0:T(8,128)S(1)}, f32[8,40,256]{2,1,0:T(8,128)S(1)}, f32[8,40,256]{2,1,0:T(8,128)S(1)}, f32[8,40,256]{2,1,0:T(8,128)S(1...) custom-call(f32[5,32,256]{2,1,0:T(8,128)S(1)} %collective-permute-done.rows_one, ...), custom_call_target="tpu_custom_call" | custom-call | flops 9830400 | bytes 8126464 | tf_op jit(solution)/shard_map/near_residual/pallas_call | solution.py:658
  24.9 0.0 collective-permute-done.2.columns_one
  24.9 0.0 collective-permute-done.3.columns_two
  24.9 2.7 %finish.1 = (f32[9,8,32,256]{3,2,1,0:T(8,128)}, f32[8,32,256]{2,1,0:T(8,128)}) custom-call(f32[40,256]{1,0:T(8,128)S(1)} %collective-permute-done.2.columns_one, f32[40,256]{1,0:T(8,128)S(1)} %collective-permute-done.3.columns_two, f32[40,512]{1,0:T(8,128)S(1)} %get-tuple-element.43.packet, f32[8,32,256]{2,1,0:T(8,128)S(1)} %copy-done, ...), custom_call_target="tpu_custom_call" | custom-call | tf_op jit(solution)/shard_map/finish/pallas_call | solution.py:675
Async XLA Ops:
  0.6 9.3 %copy-start.5 = (s32[4,8]{1,0:T(4,128)S(1)}, s32[4,8]{1,0:T(4,128)}, u32[]{:S(2)}) copy-start(s32[4,8]{1,0:T(4,128)} %flags.1) | copy-start | bytes 388
  0.6 9.3 %copy-start.7 = (f32[9]{0:T(128)S(1)}, f32[9]{0:T(128)}, u32[]{:S(2)}) copy-start(f32[9]{0:T(128)} %slope.1) | copy-start | bytes 112
  0.7 9.3 %copy-start.6 = (f32[9]{0:T(128)S(1)}, f32[9]{0:T(128)}, u32[]{:S(2)}) copy-start(f32[9]{0:T(128)} %vol.1) | copy-start | bytes 112
  6.4 4.7 %collective-permute-start = (f32[5,32,256]{2,1,0:T(8,128)S(1)}, f32[5,32,256]{2,1,0:T(8,128)S(1)}, u32[]{:S(2)}, u32[]{:S(2)}) collective-permute-start(f32[5,32,256]{2,1,0:T(8,128)S(1)} %get-tuple-element.26), channel_id=1, source_target_pairs={{0,4},{8,12},{16,20},{24,28},{4,0},{12,8},{20,16},{28,24},{1,5},{9... | collective-permute-start | bytes 491528 | tf_op jit(solution)/shard_map/ppermute | solution.py:602
  6.5 8.5 %collective-permute-start.1 = (f32[5,32,256]{2,1,0:T(8,128)S(1)}, f32[5,32,256]{2,1,0:T(8,128)S(1)}, u32[]{:S(2)}, u32[]{:S(2)}) collective-permute-start(f32[5,32,256]{2,1,0:T(8,128)S(1)} %get-tuple-element.27), channel_id=1, source_target_pairs={{4,8},{12,16},{20,24},{8,4},{16,12},{24,20},{5,9},{13,17},{21,25},... | collective-permute-start | bytes 491528 | tf_op jit(solution)/shard_map/ppermute | solution.py:602
  10.0 5.0 %copy-start = (f32[8,32,256]{2,1,0:T(8,128)S(1)}, f32[8,32,256]{2,1,0:T(8,128)}, u32[]{:S(2)}) copy-start(f32[8,32,256]{2,1,0:T(8,128)} %press.5) | copy-start | bytes 786436
  10.0 5.0 %copy-start.1 = (f32[8,32,256]{2,1,0:T(8,128)S(1)}, f32[8,32,256]{2,1,0:T(8,128)}, u32[]{:S(2)}) copy-start(f32[8,32,256]{2,1,0:T(8,128)} %pore.3) | copy-start | bytes 786436
  10.0 5.0 %copy-start.2 = (f32[8,32,256]{2,1,0:T(8,128)S(1)}, f32[8,32,256]{2,1,0:T(8,128)}, u32[]{:S(2)}) copy-start(f32[8,32,256]{2,1,0:T(8,128)} %tx.3) | copy-start | bytes 786436
  10.0 5.0 %copy-start.3 = (f32[8,32,256]{2,1,0:T(8,128)S(1)}, f32[8,32,256]{2,1,0:T(8,128)}, u32[]{:S(2)}) copy-start(f32[8,32,256]{2,1,0:T(8,128)} %ty.3) | copy-start | bytes 786436
  10.0 5.0 %copy-start.4 = (f32[8,32,256]{2,1,0:T(8,128)S(1)}, f32[8,32,256]{2,1,0:T(8,128)}, u32[]{:S(2)}) copy-start(f32[8,32,256]{2,1,0:T(8,128)} %tz.3) | copy-start | bytes 786436
  15.8 9.1 %collective-permute-start.2 = (f32[40,256]{1,0:T(8,128)S(1)}, f32[40,256]{1,0:T(8,128)S(1)}, u32[]{:S(2)}, u32[]{:S(2)}) collective-permute-start(f32[40,256]{1,0:T(8,128)S(1)} %get-tuple-element.41), channel_id=1, source_target_pairs={{0,1},{2,3},{1,0},{3,2},{4,5},{6,7},{5,4},{7,6},{8,9},{10,11},{9,8... | collective-permute-start | bytes 122888 | tf_op jit(solution)/shard_map/ppermute | solution.py:602
  16.2 8.7 %collective-permute-start.3 = (f32[40,256]{1,0:T(8,128)S(1)}, f32[40,256]{1,0:T(8,128)S(1)}, u32[]{:S(2)}, u32[]{:S(2)}) collective-permute-start(f32[40,256]{1,0:T(8,128)S(1)} %get-tuple-element.42), channel_id=1, source_target_pairs={{1,2},{2,1},{5,6},{6,5},{9,10},{10,9},{13,14},{14,13},{17,18},{18,... | collective-permute-start | bytes 122888 | tf_op jit(solution)/shard_map/ppermute | solution.py:602
where the time goes:
time: 27.5 us; the launch traced here: 27.7 us
  Pallas kernels  13.8 us (50%)
  starting transfers between devices  9.12 us (33%)
  waiting for transfers between devices  3.87 us (14%)
  between operations  0.81 us (3%)
    ppermute x4, starting transfers between devices, swapped(): return lax.ppermute(block, axis, pairs + [(j, i) for i, j in pairs])  9.12 us
    pallas_call x1, Pallas kernels, on_device(): pl.pallas_call(edge_cells, in_specs=[pl.BlockSpec(memory_space=pl.ANY)] *...  5.75 us
    ppermute x4, waiting for transfers between devices, swapped(): return lax.ppermute(block, axis, pairs + [(j, i) for i, j in pairs])  3.87 us
    pallas_call x1, Pallas kernels, on_device(): pl.pallas_call(near_residual, in_specs=[vmem] * 15, out_specs=[vmem] * 6,...  3.48 us
    pallas_call x1, Pallas kernels, on_device(): pl.pallas_call(finish, in_specs=[vmem] * 12, out_specs=[pl.BlockSpec(memo...  2.73 us
    pallas_call x1, Pallas kernels, on_device(): pl.pallas_call(inner_cells, in_specs=[smem] * 3 + [vmem] * 5, out_specs=[...  1.08 us
    pallas_call x1, Pallas kernels, on_device(): pl.pallas_call(pack_columns, in_specs=[vmem] * 15, out_specs=[vmem] * 3,...  0.79 us
  transfers between devices with their start and end apart: 4, of which 1 were waited for; matrix products, arithmetic and copies ran while one was open for 0% of the time, Pallas kernels for 16%

commit v1 on v0

--- a/solution.py
+++ b/solution.py
@@ -173,7 +173,7 @@
     return tiles
 
 
-def pack_columns(rows_one, rows_two, *refs):
+def pack_columns(rows_two, rows_one, *refs):
     (
         press, tx, ty, tz, pore, edge_mob, _, edge_mob_sum, edge_acc_sum, mob, _, mob_sum, acc_sum,
         one_ref, two_ref, own_ref,
@@ -381,7 +381,7 @@
 
 
 def near_residual(
-    rows_one, rows_two, press, tx, ty, tz, pore,
+    rows_two, rows_one, press, tx, ty, tz, pore,
     edge_mob, edge_acc, edge_mob_sum, edge_acc_sum, mob, acc, mob_sum, acc_sum,
     out_ref, total_ref, diagonal_ref, c_x, c_y, c_z,
     rows_h, fields_h, g_x, g_y, g_z,
@@ -472,7 +472,7 @@
 def finish(
     columns_one, columns_two, packet, press, total_in, diagonal_in, c_x, c_y, c_z, edge_mob, mob, near,
     res_ref, new_ref,
-    side_h, edge_h, first, total_ref, inverse_ref, res_s, sems,
+    side_h, edge_h, first, total_ref, inverse_ref, res_s, new_s, sems,
 ):
     depth, rows, width = press.shape
     layer, layers = lax.axis_index("layer"), lax.axis_size("layer")
@@ -534,7 +534,10 @@
         edge_h[which] = jnp.where(is_left, value, turned(value, -2))
 
     def leave(z):
-        return pltpu.make_async_copy(res_s.at[:, z], res_ref.at[:, z], sems.at[z])
+        return pltpu.make_async_copy(res_s.at[:, z], res_ref.at[:, z], sems.at[0, z])
+
+    def leave_new(z):
+        return pltpu.make_async_copy(new_s.at[z], new_ref.at[z], sems.at[1, z])
 
     def update(z):
         faces = [face[:rows] for face in edges(FACE, z)]
@@ -571,14 +574,16 @@
         )
         beyond = edges(NEXT, z)
         for n, span in enumerate((low, high)):
-            new_ref[z, :, span] = press[z, :, span] + inverse_ref[z, :, span] * (
+            new_s[z, :, span] = press[z, :, span] + inverse_ref[z, :, span] * (
                 gathered[:, span] + beyond[n][:rows]
             )
+        leave_new(z).start()
 
     by_pairs(depth, second)
 
     def left(z):
         leave(z).wait()
+        leave_new(z).wait()
 
     by_pairs(depth, left)
 
@@ -649,7 +654,7 @@
         out_shape=[narrow, narrow, jax.ShapeDtypeStruct((rows + ROWS, FIELDS * 32), f32)],
         compiler_params=params(24),
         name="pack_columns",
-    )(rows_one, rows_two, *planes_of, *edge, *inner)
+    )(rows_two, rows_one, *planes_of, *edge, *inner)
     columns_one = swapped(one, "layer", 0)
     columns_two = swapped(two, "layer", 1)
 
@@ -670,12 +675,12 @@
         compiler_params=params(24),
         cost_estimate=pl.CostEstimate(flops=150 * cells, transcendentals=0, bytes_accessed=4 * 31 * cells),
         name="near_residual",
-    )(rows_one, rows_two, *planes_of, *edge, *inner)
+    )(rows_two, rows_one, *planes_of, *edge, *inner)
 
     return pl.pallas_call(
         finish,
         in_specs=[vmem] * 12,
-        out_specs=[pl.BlockSpec(memory_space=pl.ANY), vmem],
+        out_specs=[pl.BlockSpec(memory_space=pl.ANY)] * 2,
         out_shape=[whole, sums],
         scratch_shapes=[
             pltpu.VMEM((COMPS, rows, LANES), f32),
@@ -684,7 +689,8 @@
             pltpu.VMEM((depth, rows, width), f32),
             pltpu.VMEM((depth, rows, width), f32),
             pltpu.VMEM((COMPS, depth, rows, width), f32),
-            pltpu.SemaphoreType.DMA((depth,)),
+            pltpu.VMEM((depth, rows, width), f32),
+            pltpu.SemaphoreType.DMA((2, depth)),
         ],
         compiler_params=params(24),
         name="finish",

time: 27.5 us -> 27.1 us (0.985); the launches traced: 27.7 us -> 26.7 us
  waiting for transfers between devices: 3.87 us -> 0.01 us
  Pallas kernels: 13.8 us -> 16.9 us
    ppermute x4, waiting for transfers between devices: 3.87 us -> 0.01 us  [swapped(): return lax.ppermute(block, axis, pairs + [(j, i) for i, j in pairs])]
    pallas_call x1, Pallas kernels: 1.08 us -> 4.91 us  [on_device(): pl.pallas_call(inner_cells, in_specs=[smem] * 3 + [vmem] * 5, out_specs=[...]
    pallas_call x1, Pallas kernels: 5.75 us -> 5.23 us  [on_device(): pl.pallas_call(edge_cells, in_specs=[pl.BlockSpec(memory_space=pl.ANY)] *...]
  transfers between devices with their start and end apart: 4 -> 4, of which waited for: 1 -> 0; matrix products, arithmetic and copies ran while one was open for 0% -> 0% of each run, Pallas kernels for 16% -> 31%
where the time goes in v1:
time: 27.1 us; the launch traced here: 26.7 us
  Pallas kernels  16.9 us (62%)
  starting transfers between devices  8.99 us (33%)
  between operations  0.8 us (3%)
    ppermute x4, starting transfers between devices, swapped(): return lax.ppermute(block, axis, pairs + [(j, i) for i, j in pairs])  8.99 us
    pallas_call x1, Pallas kernels, on_device(): pl.pallas_call(edge_cells, in_specs=[pl.BlockSpec(memory_space=pl.ANY)] *...  5.23 us
    pallas_call x1, Pallas kernels, on_device(): pl.pallas_call(inner_cells, in_specs=[smem] * 3 + [vmem] * 5, out_specs=[...  4.91 us
    pallas_call x1, Pallas kernels, on_device(): pl.pallas_call(near_residual, in_specs=[vmem] * 15, out_specs=[vmem] * 6,...  3.48 us
    pallas_call x1, Pallas kernels, on_device(): pl.pallas_call(finish, in_specs=[vmem] * 12, out_specs=[pl.BlockSpec(memo...  2.46 us
    pallas_call x1, Pallas kernels, on_device(): pl.pallas_call(pack_columns, in_specs=[vmem] * 15, out_specs=[vmem] * 3,...  0.79 us
  transfers between devices with their start and end apart: 4, of which 0 were waited for; matrix products, arithmetic and copies ran while one was open for 0% of the time, Pallas kernels for 31%

profile of v1, /device:TPU:12, one launch (start us, length us, event | category | flops | bytes accessed | tf_op | source)
XLA Modules:
  0.0 26.7 jit_solution(13457580360998886958)
XLA Ops:
  0.6 0.0 copy-start.5
  0.6 0.0 copy-start.7
  0.7 0.0 copy-start.6
  0.7 5.2 %edge_cells.1 = (f32[9,8,16,256]{3,2,1,0:T(8,128)S(1)}, f32[9,8,16,256]{3,2,1,0:T(8,128)S(1)}, f32[8,16,256]{2,1,0:T(8,128)S(1)}, f32[8,16,256]{2,1,0:T(8,128)S(...) custom-call(s32[4,8]{1,0:T(4,128)} %flags.1, ...), custom_call_target="tpu_custom_call" | custom-call | tf_op jit(solution)/shard_map/edge_cells/pallas_call | solution.py:620
  5.9 3.3 %collective-permute-start = (f32[5,32,256]{2,1,0:T(8,128)S(1)}, f32[5,32,256]{2,1,0:T(8,128)S(1)}, u32[]{:S(2)}, u32[]{:S(2)}) collective-permute-start(f32[5,32,256]{2,1,0:T(8,128)S(1)} %get-tuple-element.26), channel_id=1, source_target_pairs={{4,8},{12,16},{20,24},{8,4},{16,12},{24,20},{5,9},{13,17},{21,25},... | collective-permute-start | bytes 491528 | tf_op jit(solution)/shard_map/ppermute | solution.py:607
  9.2 0.8 %collective-permute-start.1 = (f32[5,32,256]{2,1,0:T(8,128)S(1)}, f32[5,32,256]{2,1,0:T(8,128)S(1)}, u32[]{:S(2)}, u32[]{:S(2)}) collective-permute-start(f32[5,32,256]{2,1,0:T(8,128)S(1)} %get-tuple-element.27), channel_id=1, source_target_pairs={{0,4},{8,12},{16,20},{24,28},{4,0},{12,8},{20,16},{28,24},{1,5},{9... | collective-permute-start | bytes 491528 | tf_op jit(solution)/shard_map/ppermute | solution.py:607
  10.0 0.0 copy-done.5
  10.0 0.0 copy-done.7
  10.0 0.0 copy-done.6
  10.0 0.0 copy-start
  10.0 0.0 copy-start.1
  10.0 0.0 copy-start.2
  10.0 0.0 copy-start.3
  10.1 0.0 copy-start.4
  10.1 4.9 %inner_cells.1 = (f32[9,8,16,256]{3,2,1,0:T(8,128)S(1)}, f32[9,8,16,256]{3,2,1,0:T(8,128)S(1)}, f32[8,16,256]{2,1,0:T(8,128)S(1)}, f32[8,16,256]{2,1,0:T(8,128)S(1)}) custom-call(s32[4,8]{1,0:T(4,128)S(1)} %copy-done.5, f32[9]{0:T(128)S(1)} %copy-done.6, f32[9]{0:T(128)S(1)} %copy-done.7, bf16[80,256]{1,0:T(8,128)(2,1)S(1)} %get-tuple-element.32.operand, ...), custom_call_target="tpu_custom_call" | custom-call | flops 29491200 | bytes 5111808 | tf_op jit(solution)/shard_map/inner_cells/pallas_call | solution.py:636
  15.0 0.0 collective-permute-done.rows_two
  15.0 0.0 collective-permute-done.1.rows_one
  15.0 0.0 copy-done
  15.0 0.0 copy-done.1
  15.0 0.0 copy-done.2
  15.0 0.0 copy-done.3
  15.0 0.0 copy-done.4
  15.1 0.8 %pack_columns.1 = (f32[40,256]{1,0:T(8,128)S(1)}, f32[40,256]{1,0:T(8,128)S(1)}, f32[40,512]{1,0:T(8,128)S(1)}) custom-call(f32[5,32,256]{2,1,0:T(8,128)S(1)} %collective-permute-done.rows_two, f32[5,32,256]{2,1,0:T(8,128)S(1)} %collective-permute-done.1.rows_one, f32[8,32,256]{2,1,0:T(8,128)S(1)} %copy-done, f32[8,32,256]{2,1,0:T(8,128)S(1)} %copy-done.2, ...), custom_call_target="tpu_custom_call" | custom-call | tf_op jit(solution)/shard_map/pack_columns/pallas_call | solution.py:650
  15.8 0.5 %collective-permute-start.2 = (f32[40,256]{1,0:T(8,128)S(1)}, f32[40,256]{1,0:T(8,128)S(1)}, u32[]{:S(2)}, u32[]{:S(2)}) collective-permute-start(f32[40,256]{1,0:T(8,128)S(1)} %get-tuple-element.41), channel_id=1, source_target_pairs={{0,1},{2,3},{1,0},{3,2},{4,5},{6,7},{5,4},{7,6},{8,9},{10,11},{9,8... | collective-permute-start | bytes 122888 | tf_op jit(solution)/shard_map/ppermute | solution.py:607
  16.4 4.4 %collective-permute-start.3 = (f32[40,256]{1,0:T(8,128)S(1)}, f32[40,256]{1,0:T(8,128)S(1)}, u32[]{:S(2)}, u32[]{:S(2)}) collective-permute-start(f32[40,256]{1,0:T(8,128)S(1)} %get-tuple-element.42), channel_id=1, source_target_pairs={{1,2},{2,1},{5,6},{6,5},{9,10},{10,9},{13,14},{14,13},{17,18},{18,... | collective-permute-start | bytes 122888 | tf_op jit(solution)/shard_map/ppermute | solution.py:607
  20.8 3.5 %near_residual.1 = (f32[9,8,32,256]{3,2,1,0:T(8,128)S(1)}, f32[8,40,256]{2,1,0:T(8,128)S(1)}, f32[8,40,256]{2,1,0:T(8,128)S(1)}, f32[8,40,256]{2,1,0:T(8,128)S(1...) custom-call(f32[5,32,256]{2,1,0:T(8,128)S(1)} %collective-permute-done.rows_two, ...), custom_call_target="tpu_custom_call" | custom-call | flops 9830400 | bytes 8126464 | tf_op jit(solution)/shard_map/near_residual/pallas_call | solution.py:663
  24.2 0.0 collective-permute-done.2.columns_one
  24.2 0.0 collective-permute-done.3.columns_two
  24.3 2.5 %finish.1 = (f32[9,8,32,256]{3,2,1,0:T(8,128)}, f32[8,32,256]{2,1,0:T(8,128)}) custom-call(f32[40,256]{1,0:T(8,128)S(1)} %collective-permute-done.2.columns_one, f32[40,256]{1,0:T(8,128)S(1)} %collective-permute-done.3.columns_two, f32[40,512]{1,0:T(8,128)S(1)} %get-tuple-element.43.packet, f32[8,32,256]{2,1,0:T(8,128)S(1)} %copy-done, ...), custom_call_target="tpu_custom_call" | custom-call | tf_op jit(solution)/shard_map/finish/pallas_call | solution.py:680
Async XLA Ops:
  0.6 9.4 %copy-start.5 = (s32[4,8]{1,0:T(4,128)S(1)}, s32[4,8]{1,0:T(4,128)}, u32[]{:S(2)}) copy-start(s32[4,8]{1,0:T(4,128)} %flags.1) | copy-start | bytes 388
  0.6 9.4 %copy-start.7 = (f32[9]{0:T(128)S(1)}, f32[9]{0:T(128)}, u32[]{:S(2)}) copy-start(f32[9]{0:T(128)} %slope.1) | copy-start | bytes 112
  0.7 9.4 %copy-start.6 = (f32[9]{0:T(128)S(1)}, f32[9]{0:T(128)}, u32[]{:S(2)}) copy-start(f32[9]{0:T(128)} %vol.1) | copy-start | bytes 112
  5.9 9.1 %collective-permute-start = (f32[5,32,256]{2,1,0:T(8,128)S(1)}, f32[5,32,256]{2,1,0:T(8,128)S(1)}, u32[]{:S(2)}, u32[]{:S(2)}) collective-permute-start(f32[5,32,256]{2,1,0:T(8,128)S(1)} %get-tuple-element.26), channel_id=1, source_target_pairs={{4,8},{12,16},{20,24},{8,4},{16,12},{24,20},{5,9},{13,17},{21,25},... | collective-permute-start | bytes 491528 | tf_op jit(solution)/shard_map/ppermute | solution.py:607
  9.2 5.8 %collective-permute-start.1 = (f32[5,32,256]{2,1,0:T(8,128)S(1)}, f32[5,32,256]{2,1,0:T(8,128)S(1)}, u32[]{:S(2)}, u32[]{:S(2)}) collective-permute-start(f32[5,32,256]{2,1,0:T(8,128)S(1)} %get-tuple-element.27), channel_id=1, source_target_pairs={{0,4},{8,12},{16,20},{24,28},{4,0},{12,8},{20,16},{28,24},{1,5},{9... | collective-permute-start | bytes 491528 | tf_op jit(solution)/shard_map/ppermute | solution.py:607
  10.0 5.0 %copy-start = (f32[8,32,256]{2,1,0:T(8,128)S(1)}, f32[8,32,256]{2,1,0:T(8,128)}, u32[]{:S(2)}) copy-start(f32[8,32,256]{2,1,0:T(8,128)} %press.5) | copy-start | bytes 786436
  10.0 5.0 %copy-start.1 = (f32[8,32,256]{2,1,0:T(8,128)S(1)}, f32[8,32,256]{2,1,0:T(8,128)}, u32[]{:S(2)}) copy-start(f32[8,32,256]{2,1,0:T(8,128)} %pore.3) | copy-start | bytes 786436
  10.0 5.0 %copy-start.2 = (f32[8,32,256]{2,1,0:T(8,128)S(1)}, f32[8,32,256]{2,1,0:T(8,128)}, u32[]{:S(2)}) copy-start(f32[8,32,256]{2,1,0:T(8,128)} %tx.3) | copy-start | bytes 786436
  10.0 5.0 %copy-start.3 = (f32[8,32,256]{2,1,0:T(8,128)S(1)}, f32[8,32,256]{2,1,0:T(8,128)}, u32[]{:S(2)}) copy-start(f32[8,32,256]{2,1,0:T(8,128)} %ty.3) | copy-start | bytes 786436
  10.1 5.0 %copy-start.4 = (f32[8,32,256]{2,1,0:T(8,128)S(1)}, f32[8,32,256]{2,1,0:T(8,128)}, u32[]{:S(2)}) copy-start(f32[8,32,256]{2,1,0:T(8,128)} %tz.3) | copy-start | bytes 786436
  15.8 8.4 %collective-permute-start.2 = (f32[40,256]{1,0:T(8,128)S(1)}, f32[40,256]{1,0:T(8,128)S(1)}, u32[]{:S(2)}, u32[]{:S(2)}) collective-permute-start(f32[40,256]{1,0:T(8,128)S(1)} %get-tuple-element.41), channel_id=1, source_target_pairs={{0,1},{2,3},{1,0},{3,2},{4,5},{6,7},{5,4},{7,6},{8,9},{10,11},{9,8... | collective-permute-start | bytes 122888 | tf_op jit(solution)/shard_map/ppermute | solution.py:607
  16.4 7.9 %collective-permute-start.3 = (f32[40,256]{1,0:T(8,128)S(1)}, f32[40,256]{1,0:T(8,128)S(1)}, u32[]{:S(2)}, u32[]{:S(2)}) collective-permute-start(f32[40,256]{1,0:T(8,128)S(1)} %get-tuple-element.42), channel_id=1, source_target_pairs={{1,2},{2,1},{5,6},{6,5},{9,10},{10,9},{13,14},{14,13},{17,18},{18,... | collective-permute-start | bytes 122888 | tf_op jit(solution)/shard_map/ppermute | solution.py:607

commit v2 on v1

--- a/solution.py
+++ b/solution.py
@@ -11,7 +11,7 @@
 COMPS = 9
 FIELDS = 16
 MOB, PRESS, TX, TY, TZ, PORE, ACC = range(COMPS, FIELDS)
-UNITS = (MOB, PRESS, TX, (0, 1), (2, 3), (4, 5), (6, 7), (8, TY), (TZ, PORE), (ACC, ACC))
+UNITS = ((0, 1), (2, 3), (4, 5), (6, 7), (8, MOB), (PRESS, TX), (TY, TZ), (PORE, ACC))
 DEPTH_SLOTS = 4
 TIME_STEP = 4.0
 COMPRESS = 0.2
@@ -341,12 +341,20 @@
 
         def field(k, z):
             if k < COMPS:
-                here = mob_ref[k, z, target]
-            elif k in (MOB, ACC):
-                here = (mob_sum if k == MOB else acc_sum)[z, target]
-            else:
-                here = {PRESS: press_s, TX: tx_s, TY: ty_s, TZ: tz_s, PORE: pore_s}[k][end, z]
-            return here
+                return mob_ref[k, z, target]
+            if k == MOB:
+                return mob_sum[z, target]
+            if k in (PORE, ACC):
+                m, p = mob_sum[z, target], press_s[end, z]
+                behind = ROWS - 1 if end == 0 else 1
+                strength = (0.5 * TIME_STEP) * tx_s[end, z]
+                if end == 1:
+                    strength = pltpu.roll(strength, 1, 0)
+                couple = strength * (m + pltpu.roll(m, behind, 0))
+                if k == PORE:
+                    return COMPRESS * pore_s[end, z] + couple
+                return acc_sum[z, target] + couple * (p - pltpu.roll(p, behind, 0))
+            return {PRESS: press_s, TX: tx_s, TY: ty_s, TZ: tz_s}[k][end, z]
 
         for turn, ref in enumerate((one_ref, two_ref)):
             @pl.when(odd == (end == turn))
@@ -401,7 +409,10 @@
         for i in range(COMPS):
             rows_h[i, z] = tiles[i][z]
         for n, k in enumerate(fields):
-            fields_h[n, z] = tiles[k][z]
+            tile = tiles[k][z]
+            if k == TX:
+                tile = jnp.where(row_of(tile.shape) == ROWS - 1, tile, 0.0)
+            fields_h[n, z] = tile
 
     end_x = (row_of(full) == rows - 1) & (areal == areals - 1)
     end_y = lane_of(full) == width - 1
@@ -411,7 +422,8 @@
 
     def update(z):
         m, p, x, y, zz, volume, total = (
-            jnp.concatenate([ref[z], fields_h[n, z]], axis=0) for n, ref in enumerate(fields.values())
+            jnp.concatenate([COMPRESS * ref[z] if ref is pore else ref[z], fields_h[n, z]], axis=0)
+            for n, ref in enumerate(fields.values())
         )
         up, down = jnp.minimum(z + 1, depth - 1), jnp.maximum(z - 1, 0)
         p_up = jnp.concatenate([press[up], fields_h[1, up]], axis=0)
@@ -439,7 +451,7 @@
             + (cz * dz + cz_low * (p - p_down))
         )
         diagonal_ref[z] = (
-            COMPRESS * volume
+            volume
             + (cx + pltpu.roll(cx, 1, 0))
             + (cy + pltpu.roll(cy, 1, 1))
             + (cz + cz_low)

time: 27.1 us -> 26.4 us (0.974)
  starting transfers between devices: 8.99 us -> 8.52 us
    ppermute x4, starting transfers between devices: 8.99 us -> 8.52 us  [swapped(): return lax.ppermute(block, axis, pairs + [(j, i) for i, j in pairs])]
  transfers between devices with their start and end apart: 4 -> 4, of which waited for: 0 -> 0; matrix products, arithmetic and copies ran while one was open for 0% -> 0% of each run, Pallas kernels for 31% -> 32%
where the time goes in v2:
time: 26.4 us; the launch traced here: 26.2 us
  Pallas kernels  16.8 us (64%)
  starting transfers between devices  8.52 us (32%)
  between operations  0.81 us (3%)
    ppermute x4, starting transfers between devices, swapped(): return lax.ppermute(block, axis, pairs + [(j, i) for i, j in pairs])  8.52 us
    pallas_call x1, Pallas kernels, on_device(): pl.pallas_call(edge_cells, in_specs=[pl.BlockSpec(memory_space=pl.ANY)] *...  5.25 us
    pallas_call x1, Pallas kernels, on_device(): pl.pallas_call(inner_cells, in_specs=[smem] * 3 + [vmem] * 5, out_specs=[...  4.92 us
    pallas_call x1, Pallas kernels, on_device(): pl.pallas_call(near_residual, in_specs=[vmem] * 15, out_specs=[vmem] * 6,...  3.49 us
    pallas_call x1, Pallas kernels, on_device(): pl.pallas_call(finish, in_specs=[vmem] * 12, out_specs=[pl.BlockSpec(memo...  2.4 us
    pallas_call x1, Pallas kernels, on_device(): pl.pallas_call(pack_columns, in_specs=[vmem] * 15, out_specs=[vmem] * 3,...  0.78 us
  transfers between devices with their start and end apart: 4, of which 0 were waited for; matrix products, arithmetic and copies ran while one was open for 0% of the time, Pallas kernels for 32%

profile of v2, /device:TPU:12, one launch (start us, length us, event | category | flops | bytes accessed | tf_op | source)
XLA Modules:
  0.0 26.2 jit_solution(1453627985106267958)
XLA Ops:
  0.6 0.0 copy-start.5
  0.6 0.0 copy-start.7
  0.7 0.0 copy-start.6
  0.7 5.3 %edge_cells.1 = (f32[9,8,16,256]{3,2,1,0:T(8,128)S(1)}, f32[9,8,16,256]{3,2,1,0:T(8,128)S(1)}, f32[8,16,256]{2,1,0:T(8,128)S(1)}, f32[8,16,256]{2,1,0:T(8,128)S(...) custom-call(s32[4,8]{1,0:T(4,128)} %flags.1, ...), custom_call_target="tpu_custom_call" | custom-call | tf_op jit(solution)/shard_map/edge_cells/pallas_call | solution.py:632
  5.9 3.3 %collective-permute-start = (f32[4,32,256]{2,1,0:T(8,128)S(1)}, f32[4,32,256]{2,1,0:T(8,128)S(1)}, u32[]{:S(2)}, u32[]{:S(2)}) collective-permute-start(f32[4,32,256]{2,1,0:T(8,128)S(1)} %get-tuple-element.26), channel_id=1, source_target_pairs={{4,8},{12,16},{20,24},{8,4},{16,12},{24,20},{5,9},{13,17},{21,25},... | collective-permute-start | bytes 393224 | tf_op jit(solution)/shard_map/ppermute | solution.py:619
  9.2 0.8 %collective-permute-start.1 = (f32[4,32,256]{2,1,0:T(8,128)S(1)}, f32[4,32,256]{2,1,0:T(8,128)S(1)}, u32[]{:S(2)}, u32[]{:S(2)}) collective-permute-start(f32[4,32,256]{2,1,0:T(8,128)S(1)} %get-tuple-element.27), channel_id=1, source_target_pairs={{0,4},{8,12},{16,20},{24,28},{4,0},{12,8},{20,16},{28,24},{1,5},{9... | collective-permute-start | bytes 393224 | tf_op jit(solution)/shard_map/ppermute | solution.py:619
  10.0 0.0 copy-done.5
  10.1 0.0 copy-done.7
  10.1 0.0 copy-done.6
  10.1 0.0 copy-start
  10.1 0.0 copy-start.1
  10.1 0.0 copy-start.2
  10.1 0.0 copy-start.3
  10.1 0.0 copy-start.4
  10.1 4.9 %inner_cells.1 = (f32[9,8,16,256]{3,2,1,0:T(8,128)S(1)}, f32[9,8,16,256]{3,2,1,0:T(8,128)S(1)}, f32[8,16,256]{2,1,0:T(8,128)S(1)}, f32[8,16,256]{2,1,0:T(8,128)S(1)}) custom-call(s32[4,8]{1,0:T(4,128)S(1)} %copy-done.5, f32[9]{0:T(128)S(1)} %copy-done.6, f32[9]{0:T(128)S(1)} %copy-done.7, bf16[80,256]{1,0:T(8,128)(2,1)S(1)} %get-tuple-element.32.operand, ...), custom_call_target="tpu_custom_call" | custom-call | flops 29491200 | bytes 5111808 | tf_op jit(solution)/shard_map/inner_cells/pallas_call | solution.py:648
  15.0 0.0 collective-permute-done.rows_two
  15.0 0.0 collective-permute-done.1.rows_one
  15.1 0.0 copy-done
  15.1 0.0 copy-done.1
  15.1 0.0 copy-done.2
  15.1 0.0 copy-done.3
  15.1 0.0 copy-done.4
  15.1 0.8 %pack_columns.1 = (f32[40,256]{1,0:T(8,128)S(1)}, f32[40,256]{1,0:T(8,128)S(1)}, f32[40,512]{1,0:T(8,128)S(1)}) custom-call(f32[4,32,256]{2,1,0:T(8,128)S(1)} %collective-permute-done.rows_two, f32[4,32,256]{2,1,0:T(8,128)S(1)} %collective-permute-done.1.rows_one, f32[8,32,256]{2,1,0:T(8,128)S(1)} %copy-done, f32[8,32,256]{2,1,0:T(8,128)S(1)} %copy-done.2, ...), custom_call_target="tpu_custom_call" | custom-call | tf_op jit(solution)/shard_map/pack_columns/pallas_call | solution.py:662
  15.9 0.1 collective-permute-start.2
  16.0 4.3 %collective-permute-start.3 = (f32[40,256]{1,0:T(8,128)S(1)}, f32[40,256]{1,0:T(8,128)S(1)}, u32[]{:S(2)}, u32[]{:S(2)}) collective-permute-start(f32[40,256]{1,0:T(8,128)S(1)} %get-tuple-element.42), channel_id=1, source_target_pairs={{1,2},{2,1},{5,6},{6,5},{9,10},{10,9},{13,14},{14,13},{17,18},{18,... | collective-permute-start | bytes 122888 | tf_op jit(solution)/shard_map/ppermute | solution.py:619
  20.3 3.5 %near_residual.1 = (f32[9,8,32,256]{3,2,1,0:T(8,128)S(1)}, f32[8,40,256]{2,1,0:T(8,128)S(1)}, f32[8,40,256]{2,1,0:T(8,128)S(1)}, f32[8,40,256]{2,1,0:T(8,128)S(1...) custom-call(f32[4,32,256]{2,1,0:T(8,128)S(1)} %collective-permute-done.rows_two, ...), custom_call_target="tpu_custom_call" | custom-call | flops 9830400 | bytes 8126464 | tf_op jit(solution)/shard_map/near_residual/pallas_call | solution.py:675
  23.8 0.0 collective-permute-done.2.columns_one
  23.8 0.0 collective-permute-done.3.columns_two
  23.8 2.4 %finish.1 = (f32[9,8,32,256]{3,2,1,0:T(8,128)}, f32[8,32,256]{2,1,0:T(8,128)}) custom-call(f32[40,256]{1,0:T(8,128)S(1)} %collective-permute-done.2.columns_one, f32[40,256]{1,0:T(8,128)S(1)} %collective-permute-done.3.columns_two, f32[40,512]{1,0:T(8,128)S(1)} %get-tuple-element.43.packet, f32[8,32,256]{2,1,0:T(8,128)S(1)} %copy-done, ...), custom_call_target="tpu_custom_call" | custom-call | tf_op jit(solution)/shard_map/finish/pallas_call | solution.py:692
Async XLA Ops:
  0.6 9.4 %copy-start.5 = (s32[4,8]{1,0:T(4,128)S(1)}, s32[4,8]{1,0:T(4,128)}, u32[]{:S(2)}) copy-start(s32[4,8]{1,0:T(4,128)} %flags.1) | copy-start | bytes 388
  0.6 9.4 %copy-start.7 = (f32[9]{0:T(128)S(1)}, f32[9]{0:T(128)}, u32[]{:S(2)}) copy-start(f32[9]{0:T(128)} %slope.1) | copy-start | bytes 112
  0.7 9.4 %copy-start.6 = (f32[9]{0:T(128)S(1)}, f32[9]{0:T(128)}, u32[]{:S(2)}) copy-start(f32[9]{0:T(128)} %vol.1) | copy-start | bytes 112
  5.9 9.1 %collective-permute-start = (f32[4,32,256]{2,1,0:T(8,128)S(1)}, f32[4,32,256]{2,1,0:T(8,128)S(1)}, u32[]{:S(2)}, u32[]{:S(2)}) collective-permute-start(f32[4,32,256]{2,1,0:T(8,128)S(1)} %get-tuple-element.26), channel_id=1, source_target_pairs={{4,8},{12,16},{20,24},{8,4},{16,12},{24,20},{5,9},{13,17},{21,25},... | collective-permute-start | bytes 393224 | tf_op jit(solution)/shard_map/ppermute | solution.py:619
  9.2 5.8 %collective-permute-start.1 = (f32[4,32,256]{2,1,0:T(8,128)S(1)}, f32[4,32,256]{2,1,0:T(8,128)S(1)}, u32[]{:S(2)}, u32[]{:S(2)}) collective-permute-start(f32[4,32,256]{2,1,0:T(8,128)S(1)} %get-tuple-element.27), channel_id=1, source_target_pairs={{0,4},{8,12},{16,20},{24,28},{4,0},{12,8},{20,16},{28,24},{1,5},{9... | collective-permute-start | bytes 393224 | tf_op jit(solution)/shard_map/ppermute | solution.py:619
  10.1 5.0 %copy-start = (f32[8,32,256]{2,1,0:T(8,128)S(1)}, f32[8,32,256]{2,1,0:T(8,128)}, u32[]{:S(2)}) copy-start(f32[8,32,256]{2,1,0:T(8,128)} %press.5) | copy-start | bytes 786436
  10.1 5.0 %copy-start.1 = (f32[8,32,256]{2,1,0:T(8,128)S(1)}, f32[8,32,256]{2,1,0:T(8,128)}, u32[]{:S(2)}) copy-start(f32[8,32,256]{2,1,0:T(8,128)} %pore.3) | copy-start | bytes 786436
  10.1 5.0 %copy-start.2 = (f32[8,32,256]{2,1,0:T(8,128)S(1)}, f32[8,32,256]{2,1,0:T(8,128)}, u32[]{:S(2)}) copy-start(f32[8,32,256]{2,1,0:T(8,128)} %tx.3) | copy-start | bytes 786436
  10.1 5.0 %copy-start.3 = (f32[8,32,256]{2,1,0:T(8,128)S(1)}, f32[8,32,256]{2,1,0:T(8,128)}, u32[]{:S(2)}) copy-start(f32[8,32,256]{2,1,0:T(8,128)} %ty.3) | copy-start | bytes 786436
  10.1 5.0 %copy-start.4 = (f32[8,32,256]{2,1,0:T(8,128)S(1)}, f32[8,32,256]{2,1,0:T(8,128)}, u32[]{:S(2)}) copy-start(f32[8,32,256]{2,1,0:T(8,128)} %tz.3) | copy-start | bytes 786436
  15.9 7.9 %collective-permute-start.2 = (f32[40,256]{1,0:T(8,128)S(1)}, f32[40,256]{1,0:T(8,128)S(1)}, u32[]{:S(2)}, u32[]{:S(2)}) collective-permute-start(f32[40,256]{1,0:T(8,128)S(1)} %get-tuple-element.41), channel_id=1, source_target_pairs={{0,1},{2,3},{1,0},{3,2},{4,5},{6,7},{5,4},{7,6},{8,9},{10,11},{9,8... | collective-permute-start | bytes 122888 | tf_op jit(solution)/shard_map/ppermute | solution.py:619
  16.0 7.9 %collective-permute-start.3 = (f32[40,256]{1,0:T(8,128)S(1)}, f32[40,256]{1,0:T(8,128)S(1)}, u32[]{:S(2)}, u32[]{:S(2)}) collective-permute-start(f32[40,256]{1,0:T(8,128)S(1)} %get-tuple-element.42), channel_id=1, source_target_pairs={{1,2},{2,1},{5,6},{6,5},{9,10},{10,9},{13,14},{14,13},{17,18},{18,... | collective-permute-start | bytes 122888 | tf_op jit(solution)/shard_map/ppermute | solution.py:619

commit v3 on v2

--- a/solution.py
+++ b/solution.py
@@ -482,7 +482,7 @@
 
 
 def finish(
-    columns_one, columns_two, packet, press, total_in, diagonal_in, c_x, c_y, c_z, edge_mob, mob, near,
+    columns_two, columns_one, packet, press, total_in, diagonal_in, c_x, c_y, c_z, edge_mob, mob, near,
     res_ref, new_ref,
     side_h, edge_h, first, total_ref, inverse_ref, res_s, new_s, sems,
 ):
@@ -667,8 +667,8 @@
         compiler_params=params(24),
         name="pack_columns",
     )(rows_two, rows_one, *planes_of, *edge, *inner)
+    columns_two = swapped(two, "layer", 1)
     columns_one = swapped(one, "layer", 0)
-    columns_two = swapped(two, "layer", 1)
 
     tall = jax.ShapeDtypeStruct((depth, rows + ROWS, width), f32)
     above_faces = jax.ShapeDtypeStruct((depth + 1, rows + ROWS, width), f32)
@@ -706,7 +706,7 @@
         ],
         compiler_params=params(24),
         name="finish",
-    )(columns_one, columns_two, packet, pressure, *sweep, edge[0], inner[0], near)
+    )(columns_two, columns_one, packet, pressure, *sweep, edge[0], inner[0], near)
 
 
 def solution(mesh):

time: 26.4 us -> 27.4 us (1.038)
  the two profiles are of different devices: /device:TPU:12 before, /device:TPU:2 now
where the time goes in v3:
time: 27.4 us; the launch traced here: 26.9 us
  Pallas kernels  15.4 us (56%)
  starting transfers between devices  10.6 us (39%)
  between operations  0.8 us (3%)
    ppermute x4, starting transfers between devices, swapped(): return lax.ppermute(block, axis, pairs + [(j, i) for i, j in pairs])  10.6 us
    pallas_call x1, Pallas kernels, on_device(): pl.pallas_call(edge_cells, in_specs=[pl.BlockSpec(memory_space=pl.ANY)] *...  5.79 us
    pallas_call x1, Pallas kernels, on_device(): pl.pallas_call(near_residual, in_specs=[vmem] * 15, out_specs=[vmem] * 6,...  3.47 us
    pallas_call x1, Pallas kernels, on_device(): pl.pallas_call(inner_cells, in_specs=[smem] * 3 + [vmem] * 5, out_specs=[...  3 us
    pallas_call x1, Pallas kernels, on_device(): pl.pallas_call(finish, in_specs=[vmem] * 12, out_specs=[pl.BlockSpec(memo...  2.4 us
    pallas_call x1, Pallas kernels, on_device(): pl.pallas_call(pack_columns, in_specs=[vmem] * 15, out_specs=[vmem] * 3,...  0.78 us
  transfers between devices with their start and end apart: 4, of which 0 were waited for; matrix products, arithmetic and copies ran while one was open for 0% of the time, Pallas kernels for 24%

profile of v3, /device:TPU:2, one launch (start us, length us, event | category | flops | bytes accessed | tf_op | source)
XLA Modules:
  0.0 26.9 jit_solution(10589161890950784475)
XLA Ops:
  0.6 0.0 copy-start.5
  0.6 0.0 copy-start.7
  0.7 0.0 copy-start.6
  0.7 5.8 %edge_cells.1 = (f32[9,8,16,256]{3,2,1,0:T(8,128)S(1)}, f32[9,8,16,256]{3,2,1,0:T(8,128)S(1)}, f32[8,16,256]{2,1,0:T(8,128)S(1)}, f32[8,16,256]{2,1,0:T(8,128)S(...) custom-call(s32[4,8]{1,0:T(4,128)} %flags.1, ...), custom_call_target="tpu_custom_call" | custom-call | tf_op jit(solution)/shard_map/edge_cells/pallas_call | solution.py:632
  6.5 1.9 %collective-permute-start = (f32[4,32,256]{2,1,0:T(8,128)S(1)}, f32[4,32,256]{2,1,0:T(8,128)S(1)}, u32[]{:S(2)}, u32[]{:S(2)}) collective-permute-start(f32[4,32,256]{2,1,0:T(8,128)S(1)} %get-tuple-element.26), channel_id=1, source_target_pairs={{4,8},{12,16},{20,24},{8,4},{16,12},{24,20},{5,9},{13,17},{21,25},... | collective-permute-start | bytes 393224 | tf_op jit(solution)/shard_map/ppermute | solution.py:619
  8.4 1.7 %collective-permute-start.1 = (f32[4,32,256]{2,1,0:T(8,128)S(1)}, f32[4,32,256]{2,1,0:T(8,128)S(1)}, u32[]{:S(2)}, u32[]{:S(2)}) collective-permute-start(f32[4,32,256]{2,1,0:T(8,128)S(1)} %get-tuple-element.27), channel_id=1, source_target_pairs={{0,4},{8,12},{16,20},{24,28},{4,0},{12,8},{20,16},{28,24},{1,5},{9... | collective-permute-start | bytes 393224 | tf_op jit(solution)/shard_map/ppermute | solution.py:619
  10.0 0.0 copy-done.5
  10.0 0.0 copy-done.7
  10.1 0.0 copy-done.6
  10.1 0.0 copy-start
  10.1 0.0 copy-start.1
  10.1 0.0 copy-start.2
  10.1 0.0 copy-start.3
  10.1 0.0 copy-start.4
  10.1 3.0 %inner_cells.1 = (f32[9,8,16,256]{3,2,1,0:T(8,128)S(1)}, f32[9,8,16,256]{3,2,1,0:T(8,128)S(1)}, f32[8,16,256]{2,1,0:T(8,128)S(1)}, f32[8,16,256]{2,1,0:T(8,128)S(1)}) custom-call(s32[4,8]{1,0:T(4,128)S(1)} %copy-done.5, f32[9]{0:T(128)S(1)} %copy-done.6, f32[9]{0:T(128)S(1)} %copy-done.7, bf16[80,256]{1,0:T(8,128)(2,1)S(1)} %get-tuple-element.32.operand, ...), custom_call_target="tpu_custom_call" | custom-call | flops 29491200 | bytes 5111808 | tf_op jit(solution)/shard_map/inner_cells/pallas_call | solution.py:648
  13.1 0.0 collective-permute-done.rows_two
  13.1 0.0 collective-permute-done.1.rows_one
  13.1 0.0 copy-done
  13.2 0.0 copy-done.1
  13.2 0.0 copy-done.2
  13.2 0.0 copy-done.3
  13.2 0.0 copy-done.4
  13.2 0.8 %pack_columns.1 = (f32[40,256]{1,0:T(8,128)S(1)}, f32[40,256]{1,0:T(8,128)S(1)}, f32[40,512]{1,0:T(8,128)S(1)}) custom-call(f32[4,32,256]{2,1,0:T(8,128)S(1)} %collective-permute-done.rows_two, f32[4,32,256]{2,1,0:T(8,128)S(1)} %collective-permute-done.1.rows_one, f32[8,32,256]{2,1,0:T(8,128)S(1)} %copy-done, f32[8,32,256]{2,1,0:T(8,128)S(1)} %copy-done.2, ...), custom_call_target="tpu_custom_call" | custom-call | tf_op jit(solution)/shard_map/pack_columns/pallas_call | solution.py:662
  14.0 0.7 %collective-permute-start.2 = (f32[40,256]{1,0:T(8,128)S(1)}, f32[40,256]{1,0:T(8,128)S(1)}, u32[]{:S(2)}, u32[]{:S(2)}) collective-permute-start(f32[40,256]{1,0:T(8,128)S(1)} %get-tuple-element.41), channel_id=1, source_target_pairs={{1,2},{2,1},{5,6},{6,5},{9,10},{10,9},{13,14},{14,13},{17,18},{18,... | collective-permute-start | bytes 122888 | tf_op jit(solution)/shard_map/ppermute | solution.py:619
  14.6 6.4 %collective-permute-start.3 = (f32[40,256]{1,0:T(8,128)S(1)}, f32[40,256]{1,0:T(8,128)S(1)}, u32[]{:S(2)}, u32[]{:S(2)}) collective-permute-start(f32[40,256]{1,0:T(8,128)S(1)} %get-tuple-element.42), channel_id=1, source_target_pairs={{0,1},{2,3},{1,0},{3,2},{4,5},{6,7},{5,4},{7,6},{8,9},{10,11},{9,8... | collective-permute-start | bytes 122888 | tf_op jit(solution)/shard_map/ppermute | solution.py:619
  21.0 3.5 %near_residual.1 = (f32[9,8,32,256]{3,2,1,0:T(8,128)S(1)}, f32[8,40,256]{2,1,0:T(8,128)S(1)}, f32[8,40,256]{2,1,0:T(8,128)S(1)}, f32[8,40,256]{2,1,0:T(8,128)S(1...) custom-call(f32[4,32,256]{2,1,0:T(8,128)S(1)} %collective-permute-done.rows_two, ...), custom_call_target="tpu_custom_call" | custom-call | flops 9830400 | bytes 8126464 | tf_op jit(solution)/shard_map/near_residual/pallas_call | solution.py:675
  24.5 0.0 collective-permute-done.2.columns_two
  24.5 0.0 collective-permute-done.3.columns_one
  24.5 2.4 %finish.1 = (f32[9,8,32,256]{3,2,1,0:T(8,128)}, f32[8,32,256]{2,1,0:T(8,128)}) custom-call(f32[40,256]{1,0:T(8,128)S(1)} %collective-permute-done.2.columns_two, f32[40,256]{1,0:T(8,128)S(1)} %collective-permute-done.3.columns_one, f32[40,512]{1,0:T(8,128)S(1)} %get-tuple-element.43.packet, f32[8,32,256]{2,1,0:T(8,128)S(1)} %copy-done, ...), custom_call_target="tpu_custom_call" | custom-call | tf_op jit(solution)/shard_map/finish/pallas_call | solution.py:692
Async XLA Ops:
  0.6 9.4 %copy-start.5 = (s32[4,8]{1,0:T(4,128)S(1)}, s32[4,8]{1,0:T(4,128)}, u32[]{:S(2)}) copy-start(s32[4,8]{1,0:T(4,128)} %flags.1) | copy-start | bytes 388
  0.6 9.4 %copy-start.7 = (f32[9]{0:T(128)S(1)}, f32[9]{0:T(128)}, u32[]{:S(2)}) copy-start(f32[9]{0:T(128)} %slope.1) | copy-start | bytes 112
  0.7 9.4 %copy-start.6 = (f32[9]{0:T(128)S(1)}, f32[9]{0:T(128)}, u32[]{:S(2)}) copy-start(f32[9]{0:T(128)} %vol.1) | copy-start | bytes 112
  6.5 6.7 %collective-permute-start = (f32[4,32,256]{2,1,0:T(8,128)S(1)}, f32[4,32,256]{2,1,0:T(8,128)S(1)}, u32[]{:S(2)}, u32[]{:S(2)}) collective-permute-start(f32[4,32,256]{2,1,0:T(8,128)S(1)} %get-tuple-element.26), channel_id=1, source_target_pairs={{4,8},{12,16},{20,24},{8,4},{16,12},{24,20},{5,9},{13,17},{21,25},... | collective-permute-start | bytes 393224 | tf_op jit(solution)/shard_map/ppermute | solution.py:619
  8.4 4.7 %collective-permute-start.1 = (f32[4,32,256]{2,1,0:T(8,128)S(1)}, f32[4,32,256]{2,1,0:T(8,128)S(1)}, u32[]{:S(2)}, u32[]{:S(2)}) collective-permute-start(f32[4,32,256]{2,1,0:T(8,128)S(1)} %get-tuple-element.27), channel_id=1, source_target_pairs={{0,4},{8,12},{16,20},{24,28},{4,0},{12,8},{20,16},{28,24},{1,5},{9... | collective-permute-start | bytes 393224 | tf_op jit(solution)/shard_map/ppermute | solution.py:619
  10.1 3.1 %copy-start = (f32[8,32,256]{2,1,0:T(8,128)S(1)}, f32[8,32,256]{2,1,0:T(8,128)}, u32[]{:S(2)}) copy-start(f32[8,32,256]{2,1,0:T(8,128)} %press.5) | copy-start | bytes 786436
  10.1 3.1 %copy-start.1 = (f32[8,32,256]{2,1,0:T(8,128)S(1)}, f32[8,32,256]{2,1,0:T(8,128)}, u32[]{:S(2)}) copy-start(f32[8,32,256]{2,1,0:T(8,128)} %pore.3) | copy-start | bytes 786436
  10.1 3.1 %copy-start.2 = (f32[8,32,256]{2,1,0:T(8,128)S(1)}, f32[8,32,256]{2,1,0:T(8,128)}, u32[]{:S(2)}) copy-start(f32[8,32,256]{2,1,0:T(8,128)} %tx.3) | copy-start | bytes 786436
  10.1 3.1 %copy-start.3 = (f32[8,32,256]{2,1,0:T(8,128)S(1)}, f32[8,32,256]{2,1,0:T(8,128)}, u32[]{:S(2)}) copy-start(f32[8,32,256]{2,1,0:T(8,128)} %ty.3) | copy-start | bytes 786436
  10.1 3.1 %copy-start.4 = (f32[8,32,256]{2,1,0:T(8,128)S(1)}, f32[8,32,256]{2,1,0:T(8,128)}, u32[]{:S(2)}) copy-start(f32[8,32,256]{2,1,0:T(8,128)} %tz.3) | copy-start | bytes 786436
  14.0 10.5 %collective-permute-start.2 = (f32[40,256]{1,0:T(8,128)S(1)}, f32[40,256]{1,0:T(8,128)S(1)}, u32[]{:S(2)}, u32[]{:S(2)}) collective-permute-start(f32[40,256]{1,0:T(8,128)S(1)} %get-tuple-element.41), channel_id=1, source_target_pairs={{1,2},{2,1},{5,6},{6,5},{9,10},{10,9},{13,14},{14,13},{17,18},{18,... | collective-permute-start | bytes 122888 | tf_op jit(solution)/shard_map/ppermute | solution.py:619
  14.6 9.9 %collective-permute-start.3 = (f32[40,256]{1,0:T(8,128)S(1)}, f32[40,256]{1,0:T(8,128)S(1)}, u32[]{:S(2)}, u32[]{:S(2)}) collective-permute-start(f32[40,256]{1,0:T(8,128)S(1)} %get-tuple-element.42), channel_id=1, source_target_pairs={{0,1},{2,3},{1,0},{3,2},{4,5},{6,7},{5,4},{7,6},{8,9},{10,11},{9,8... | collective-permute-start | bytes 122888 | tf_op jit(solution)/shard_map/ppermute | solution.py:619
